TPU v7x, 256 devices: a whole 4x4x8 slice. The times are simulated.
256 devices in a mesh: dp: 256 (over z, x, y, core).
Axes of the slice: x: 4, y: 4, z: 8, core: 2. Of those that a mesh axis runs over, the one named last changes fastest.
Arguments:
- img_feat: bfloat16 [40960, 1152], P('dp'), may hold values from -24 to 24
- txt_feat: bfloat16 [40960, 1152], P('dp'), may hold values from -24 to 24
- img_head: bfloat16 [1152, 1152], replicated, may hold values from -0.1875 to 0.1875
- txt_head: bfloat16 [1152, 1152], replicated, may hold values from -0.1875 to 0.1875
- log_scale: float32 [1], replicated, may hold values from 2 to 3
- logit_bias: float32 [1], replicated, may hold values from -4 to 0
- masks: int32 [2], replicated, may hold values from 1 to 255, as said below
Outputs:
- head_grads: float32 [20736, 128], P('dp')
Inputs may be any that keep to these rules, and one draw needn't show every extreme that they name: masks[k] XOR a group's number is its partner group in round k; the 2 masks are distinct.
All inputs are finite; a program needn't handle non-finite values.
Results may differ from a plain program's by a relative error of at most 0.0065.
Values may be sent and summed in bfloat16 or wider, within the bound.
No kernel may reach another device: no remote copies, remote signals or barrier semaphores. Data moves between devices by JAX's collectives and lax.ppermute only.
A program may use at most 128 MiB of HBM per device.

v0:
```python
import jax
import jax.numpy as jnp
from jax import lax
from jax.sharding import PartitionSpec as P

EPS = 1e-06


def from_partner(block, axis, stride):
    count = lax.axis_size(axis)
    route = []
    for low in range(count):
        high = low | 1 << stride
        if high != low and high < count:
            route += [(low, high), (high, low)]
    return lax.ppermute(block, axis, route)


def normalize(y):
    r = lax.rsqrt(jnp.sum(y * y, axis=-1, keepdims=True) + EPS)
    return (y * r, r)


def block_terms(zrows, zcols, scale, bias, pos):
    cosine = lax.dot_general(
        zrows, zcols, (((1,), (1,)), ((), ())), preferred_element_type=jnp.float32
    )
    logits = scale * cosine + bias
    diff = jax.nn.sigmoid(logits) - pos
    grad_b = (diff / 16.0).astype(jnp.bfloat16)
    dz_rows = scale * jnp.dot(grad_b, zcols, preferred_element_type=jnp.float32)
    dz_cols = scale * lax.dot_general(
        grad_b, zrows, (((0,), (0,)), ((), ())), preferred_element_type=jnp.float32
    )
    return (dz_rows, dz_cols)


def backnorm(dz, z, r):
    return r * (dz - z * jnp.sum(z * dz, axis=-1, keepdims=True))


def head_grad(feat, dy):
    return lax.dot_general(
        feat, dy.astype(jnp.bfloat16), (((0,), (0,)), ((), ())), preferred_element_type=jnp.float32
    )


def bit_flag(mask, bit):
    return mask // (1 << bit) % 2 == 1


def send_texts(payload, mask, nbits):
    for bit in range(nbits):
        moved = from_partner(payload, "dp", bit)
        payload = jnp.where(bit_flag(mask, bit), moved, payload)
    return payload


def send_grads(payload, mask, nbits):
    for bit in range(nbits):
        moved = from_partner(payload.astype(jnp.bfloat16), "dp", bit).astype(payload.dtype)
        payload = jnp.where(bit_flag(mask, bit), moved, payload)
    return payload


def shards(img_feat, txt_feat, img_head, txt_head, log_scale, logit_bias, masks):
    rows = img_feat.shape[0]
    width = img_feat.shape[1]
    yi = jnp.dot(img_feat, img_head, preferred_element_type=jnp.float32)
    yt = jnp.dot(txt_feat, txt_head, preferred_element_type=jnp.float32)
    zi, ri = normalize(yi)
    zt, rt = normalize(yt)
    zib = zi.astype(jnp.bfloat16)
    ztb = zt.astype(jnp.bfloat16)
    scale = jnp.exp(log_scale[0])
    bias = logit_bias[0]
    nbits = lax.axis_size("dp").bit_length() - 1
    diagonal = jnp.eye(rows, dtype=jnp.float32)
    blank = jnp.zeros((rows, rows), jnp.float32)
    dzi, dzt = block_terms(zib, ztb, scale, bias, diagonal)
    for rnd in range(masks.shape[0]):
        mask = masks[rnd]
        partner_z = send_texts(ztb, mask, nbits)
        dz_rows, dz_cols = block_terms(zib, partner_z, scale, bias, blank)
        dzi = dzi + dz_rows
        dzt = dzt + send_grads(dz_cols, mask, nbits)
    dyi = backnorm(dzi, zi, ri)
    dyt = backnorm(dzt, zt, rt)
    grad_img = head_grad(img_feat, dyi)
    grad_txt = head_grad(txt_feat, dyt)
    stacked = jnp.stack([grad_img, grad_txt]).reshape(2 * width * width // 128, 128)
    return lax.psum_scatter(stacked, "dp", scatter_dimension=0, tiled=True)


def solution(mesh):
    return jax.shard_map(
        shards,
        mesh=mesh,
        in_specs=(P("dp", None), P("dp", None), P(), P(), P(), P(), P()),
        out_specs=P("dp", None),
        check_vma=False,
    )
```

profile of v0, /device:TPU:0, one launch (start us, length us, event | category | flops | bytes accessed | tf_op | source)
XLA Modules:
  0.0 1418.9 jit_solution(14202371819700799198)
XLA Ops:
  17.6 7.2 collective-permute-done.1
  27.4 5.2 collective-permute-done.8
  34.2 7.0 collective-permute-done.2
  42.9 5.9 collective-permute-done.9
  51.3 3.1 collective-permute-start.4
  54.3 6.0 collective-permute-done.10
  60.4 3.1 collective-permute-start.11
  63.5 6.9 collective-permute-done.4
  72.5 4.6 collective-permute-done.11
  79.2 3.4 collective-permute-start.6
  82.6 11.7 collective-permute-done.12
  95.4 18.6 %collective-permute-done.6 = bf16[160,1152]{1,0:T(8,128)(2,1)S(1)} collective-permute-done((bf16[160,1152]{1,0:T(8,128)(2,1)S(1)}, bf16[160,1152]{1,0:T(8,128)(2,1)S(1)}, u32[]{:S(2)}, u32[]{:S(2)}) %collective-permute-start.6) | collective-permute-done | bytes 368672 | tf_op jit(solution)/shard_map/ppermute | solution.py:16
  114.0 6.3 collective-permute-start.7
  121.6 13.8 collective-permute-start.14
  136.4 15.0 %collective-permute-done.14 = bf16[160,1152]{1,0:T(8,128)(2,1)S(1)} collective-permute-done((bf16[160,1152]{1,0:T(8,128)(2,1)S(1)}, bf16[160,1152]{1,0:T(8,128)(2,1)S(1)}, u32[]{:S(2)}, u32[]{:S(2)}) %collective-permute-start.14) | collective-permute-done | bytes 368672 | tf_op jit(solution)/shard_map/ppermute | solution.py:16
  152.0 13.6 collective-permute-start.23
  168.3 9.3 collective-permute-done.16
  179.3 6.3 collective-permute-done.24
  187.2 6.9 collective-permute-done.17
  195.7 5.5 collective-permute-done.25
  203.3 3.1 collective-permute-start.19
  206.4 6.4 collective-permute-done.26
  213.0 3.1 collective-permute-start.27
  216.1 6.8 collective-permute-done.19
  224.8 4.3 collective-permute-done.27
  234.1 12.2 collective-permute-done.28
  249.0 21.8 %collective-permute-start.22 = (bf16[160,1152]{1,0:T(8,128)(2,1)S(1)}, bf16[160,1152]{1,0:T(8,128)(2,1)S(1)}, u32[]{:S(2)}, u32[]{:S(2)}) collective-permute-start(bf16[160,1152]{1,0:T(8,128)(2,1)S(1)} %fusion.27), channel_id=1, source_target_pairs={{0,128},{128,0},{1,129},{129,1},{2,130},{130,2},{3,131},{131,3},{4... | collective-permute-start | bytes 1105928 | tf_op jit(solution)/shard_map/ppermute | solution.py:16
  272.8 10.8 collective-permute-start.30
  285.1 15.4 %collective-permute-done.30 = bf16[160,1152]{1,0:T(8,128)(2,1)S(1)} collective-permute-done((bf16[160,1152]{1,0:T(8,128)(2,1)S(1)}, bf16[160,1152]{1,0:T(8,128)(2,1)S(1)}, u32[]{:S(2)}, u32[]{:S(2)}) %collective-permute-start.30) | collective-permute-done | bytes 368672 | tf_op jit(solution)/shard_map/ppermute | solution.py:16
  302.0 4.6 pad_maximum_fusion
  306.6 12.7 copy.9
  319.3 11.4 reshape.18
  330.7 709.8 %fusion = f32[96,128]{1,0:T(8,128)S(1)} fusion(f32[20736,128]{1,0:T(8,128)} %reshape.18), kind=kCustom, calls=%all-reduce-scatter | all-reduce-scatter fusion | flops 3145729 | bytes 10665984
  1040.5 8.1 collective-permute-start.31
  1048.6 13.1 collective-permute-start.32
  1061.7 13.1 collective-permute-start.33
  1074.9 13.1 collective-permute-start.34
  1088.0 3.6 collective-permute-start.70
  1092.7 16.6 %collective-permute-start.35 = (f32[96,128]{1,0:T(8,128)S(1)}, f32[96,128]{1,0:T(8,128)S(1)}, u32[]{:S(2)}, u32[]{:S(2)}) collective-permute-start(f32[96,128]{1,0:T(8,128)S(1)} %fusion), channel_id=1, source_target_pairs={{0,5},{1,6},{2,7},{3,8},{4,9},{5,10},{6,11},{7,12},{8,13},{9,14},{... | collective-permute-start | bytes 147464
  1109.3 13.1 collective-permute-start.36
  1122.4 13.1 collective-permute-start.37
  1135.6 13.1 collective-permute-start.38
  1148.7 13.1 collective-permute-start.39
  1161.9 13.1 collective-permute-start.40
  1175.0 13.1 collective-permute-start.41
  1188.1 13.1 collective-permute-start.42
  1201.3 13.1 collective-permute-start.43
  1214.4 13.1 collective-permute-start.44
  1227.6 13.1 collective-permute-start.45
  1240.7 13.1 collective-permute-start.46
  1253.8 13.1 collective-permute-start.47
  1267.0 13.1 collective-permute-start.48
  1280.1 13.1 collective-permute-start.49
  1293.3 5.8 collective-permute-start.50
  1302.1 6.3 collective-permute-start.52
  1308.5 3.9 collective-permute-start.53
  1312.4 4.8 collective-permute-start.54
  1317.2 3.1 collective-permute-start.55
  1322.9 5.3 collective-permute-start.57
  1328.3 5.0 collective-permute-start.58
  1333.3 3.2 collective-permute-start.59
  1336.5 3.8 collective-permute-start.60
  1348.9 3.5 collective-permute-start.66
  1360.2 57.3 %concatenate = f32[3921,128]{1,0:T(8,128)} concatenate(f32[81,128]{1,0:T(8,128)} %collective-permute-done.70, f32[96,128]{1,0:T(8,128)} %collective-permute-done.69, f32[96,128]{1,0:T(8,128)} %collective-permute-done.68, f32[96,128]{1,0:T(8,128)} %collective-permute-done.67, f32[96,128]{1,0:T(8,128)} %collective-permute-done.66, f32[96,128]{1,0:T(8,128)} %collective-permute-done.65, ...), dimensions={0} | concatenate | bytes 4015104
  (177 shorter events, 75.5 us)
Async XLA Ops:
  13.1 11.7 collective-permute-start.1
  15.5 17.1 %collective-permute-start.8 = (bf16[160,1152]{1,0:T(8,128)(2,1)}, bf16[160,1152]{1,0:T(8,128)(2,1)S(1)}, u32[]{:S(2)}, u32[]{:S(2)}) collective-permute-start(bf16[160,1152]{1,0:T(8,128)(2,1)} %get-tuple-element.20), channel_id=1, source_target_pairs={{0,2},{2,0},{1,3},{3,1},{4,6},{6,4},{5,7},{7,5},{8,10},{10,8},{9,1... | collective-permute-start | bytes 1105928 | tf_op jit(solution)/shard_map/ppermute | solution.py:16
  25.9 15.4 %collective-permute-start.2 = (bf16[160,1152]{1,0:T(8,128)(2,1)S(1)}, bf16[160,1152]{1,0:T(8,128)(2,1)S(1)}, u32[]{:S(2)}, u32[]{:S(2)}) collective-permute-start(bf16[160,1152]{1,0:T(8,128)(2,1)S(1)} %broadcast_select_fusion.9), channel_id=1, source_target_pairs={{0,4},{4,0},{1,5},{5,1},{2,6},{6,2},{3,7},{7,3},{8,12},{12,8},{9,1... | collective-permute-start | bytes 1105928 | tf_op jit(solution)/shard_map/ppermute | solution.py:16
  32.7 16.1 %collective-permute-start.9 = (bf16[160,1152]{1,0:T(8,128)(2,1)S(1)}, bf16[160,1152]{1,0:T(8,128)(2,1)S(1)}, u32[]{:S(2)}, u32[]{:S(2)}) collective-permute-start(bf16[160,1152]{1,0:T(8,128)(2,1)S(1)} %broadcast_select_fusion.1), channel_id=1, source_target_pairs={{0,4},{4,0},{1,5},{5,1},{2,6},{6,2},{3,7},{7,3},{8,12},{12,8},{9,1... | collective-permute-start | bytes 1105928 | tf_op jit(solution)/shard_map/ppermute | solution.py:16
  41.3 9.9 collective-permute-start.3
  48.8 11.6 collective-permute-start.10
  51.3 19.2 %collective-permute-start.4 = (bf16[160,1152]{1,0:T(8,128)(2,1)S(1)}, bf16[160,1152]{1,0:T(8,128)(2,1)S(1)}, u32[]{:S(2)}, u32[]{:S(2)}) collective-permute-start(bf16[160,1152]{1,0:T(8,128)(2,1)S(1)} %broadcast_select_fusion.11), channel_id=1, source_target_pairs={{0,16},{16,0},{1,17},{17,1},{2,18},{18,2},{3,19},{19,3},{4,20},{20... | collective-permute-start | bytes 1105928 | tf_op jit(solution)/shard_map/ppermute | solution.py:16
  60.4 16.7 %collective-permute-start.11 = (bf16[160,1152]{1,0:T(8,128)(2,1)S(1)}, bf16[160,1152]{1,0:T(8,128)(2,1)S(1)}, u32[]{:S(2)}, u32[]{:S(2)}) collective-permute-start(bf16[160,1152]{1,0:T(8,128)(2,1)S(1)} %broadcast_select_fusion.3), channel_id=1, source_target_pairs={{0,16},{16,0},{1,17},{17,1},{2,18},{18,2},{3,19},{19,3},{4,20},{20... | collective-permute-start | bytes 1105928 | tf_op jit(solution)/shard_map/ppermute | solution.py:16
  70.5 8.6 collective-permute-start.5
  77.2 17.1 %collective-permute-start.12 = (bf16[160,1152]{1,0:T(8,128)(2,1)S(1)}, bf16[160,1152]{1,0:T(8,128)(2,1)S(1)}, u32[]{:S(2)}, u32[]{:S(2)}) collective-permute-start(bf16[160,1152]{1,0:T(8,128)(2,1)S(1)} %broadcast_select_fusion.4), channel_id=1, source_target_pairs={{0,32},{32,0},{1,33},{33,1},{2,34},{34,2},{3,35},{35,3},{4,36},{36... | collective-permute-start | bytes 1105928 | tf_op jit(solution)/shard_map/ppermute | solution.py:16
  79.2 34.7 %collective-permute-start.6 = (bf16[160,1152]{1,0:T(8,128)(2,1)S(1)}, bf16[160,1152]{1,0:T(8,128)(2,1)S(1)}, u32[]{:S(2)}, u32[]{:S(2)}) collective-permute-start(bf16[160,1152]{1,0:T(8,128)(2,1)S(1)} %broadcast_select_fusion.13), channel_id=1, source_target_pairs={{0,64},{64,0},{1,65},{65,1},{2,66},{66,2},{3,67},{67,3},{4,68},{68... | collective-permute-start | bytes 1105928 | tf_op jit(solution)/shard_map/ppermute | solution.py:16
  94.3 27.3 %collective-permute-start.13 = (bf16[160,1152]{1,0:T(8,128)(2,1)S(1)}, bf16[160,1152]{1,0:T(8,128)(2,1)S(1)}, u32[]{:S(2)}, u32[]{:S(2)}) collective-permute-start(bf16[160,1152]{1,0:T(8,128)(2,1)S(1)} %broadcast_select_fusion.5), channel_id=1, source_target_pairs={{0,64},{64,0},{1,65},{65,1},{2,66},{66,2},{3,67},{67,3},{4,68},{68... | collective-permute-start | bytes 1105928 | tf_op jit(solution)/shard_map/ppermute | solution.py:16
  114.0 21.5 %collective-permute-start.7 = (bf16[160,1152]{1,0:T(8,128)(2,1)S(1)}, bf16[160,1152]{1,0:T(8,128)(2,1)S(1)}, u32[]{:S(2)}, u32[]{:S(2)}) collective-permute-start(bf16[160,1152]{1,0:T(8,128)(2,1)S(1)} %broadcast_select_fusion.14), channel_id=1, source_target_pairs={{0,128},{128,0},{1,129},{129,1},{2,130},{130,2},{3,131},{131,3},{4... | collective-permute-start | bytes 1105928 | tf_op jit(solution)/shard_map/ppermute | solution.py:16
  121.6 29.7 %collective-permute-start.14 = (bf16[160,1152]{1,0:T(8,128)(2,1)S(1)}, bf16[160,1152]{1,0:T(8,128)(2,1)S(1)}, u32[]{:S(2)}, u32[]{:S(2)}) collective-permute-start(bf16[160,1152]{1,0:T(8,128)(2,1)S(1)} %broadcast_select_fusion.6), channel_id=1, source_target_pairs={{0,128},{128,0},{1,129},{129,1},{2,130},{130,2},{3,131},{131,3},{4... | collective-permute-start | bytes 1105928 | tf_op jit(solution)/shard_map/ppermute | solution.py:16
  136.1 29.9 %collective-permute-start.15 = (bf16[160,1152]{1,0:T(8,128)(2,1)S(1)}, bf16[160,1152]{1,0:T(8,128)(2,1)S(1)}, u32[]{:S(2)}, u32[]{:S(2)}) collective-permute-start(bf16[160,1152]{1,0:T(8,128)(2,1)S(1)} %get-tuple-element.29), channel_id=1, source_target_pairs={{0,1},{1,0},{2,3},{3,2},{4,5},{5,4},{6,7},{7,6},{8,9},{9,8},{10,11... | collective-permute-start | bytes 1105928 | tf_op jit(solution)/shard_map/ppermute | solution.py:16
  152.0 14.9 %collective-permute-start.23 = (bf16[160,1152]{1,0:T(8,128)(2,1)S(1)}, bf16[160,1152]{1,0:T(8,128)(2,1)S(1)}, u32[]{:S(2)}, u32[]{:S(2)}) collective-permute-start(bf16[160,1152]{1,0:T(8,128)(2,1)S(1)} %get-tuple-element.27), channel_id=1, source_target_pairs={{0,1},{1,0},{2,3},{3,2},{4,5},{5,4},{6,7},{7,6},{8,9},{9,8},{10,11... | collective-permute-start | bytes 1105928 | tf_op jit(solution)/shard_map/ppermute | solution.py:16
  166.0 11.6 collective-permute-start.16
  167.0 18.5 %collective-permute-start.24 = (bf16[160,1152]{1,0:T(8,128)(2,1)S(1)}, bf16[160,1152]{1,0:T(8,128)(2,1)S(1)}, u32[]{:S(2)}, u32[]{:S(2)}) collective-permute-start(bf16[160,1152]{1,0:T(8,128)(2,1)S(1)} %fusion.28), channel_id=1, source_target_pairs={{0,2},{2,0},{1,3},{3,1},{4,6},{6,4},{5,7},{7,5},{8,10},{10,8},{9,1... | collective-permute-start | bytes 1105928 | tf_op jit(solution)/shard_map/ppermute | solution.py:16
  177.8 16.3 %collective-permute-start.17 = (bf16[160,1152]{1,0:T(8,128)(2,1)S(1)}, bf16[160,1152]{1,0:T(8,128)(2,1)S(1)}, u32[]{:S(2)}, u32[]{:S(2)}) collective-permute-start(bf16[160,1152]{1,0:T(8,128)(2,1)S(1)} %get-tuple-element.11), channel_id=1, source_target_pairs={{0,4},{4,0},{1,5},{5,1},{2,6},{6,2},{3,7},{7,3},{8,12},{12,8},{9,1... | collective-permute-start | bytes 1105928 | tf_op jit(solution)/shard_map/ppermute | solution.py:16
  185.7 15.5 %collective-permute-start.25 = (bf16[160,1152]{1,0:T(8,128)(2,1)S(1)}, bf16[160,1152]{1,0:T(8,128)(2,1)S(1)}, u32[]{:S(2)}, u32[]{:S(2)}) collective-permute-start(bf16[160,1152]{1,0:T(8,128)(2,1)S(1)} %get-tuple-element.17), channel_id=1, source_target_pairs={{0,4},{4,0},{1,5},{5,1},{2,6},{6,2},{3,7},{7,3},{8,12},{12,8},{9,1... | collective-permute-start | bytes 1105928 | tf_op jit(solution)/shard_map/ppermute | solution.py:16
  194.1 9.1 collective-permute-start.18
  201.2 11.6 collective-permute-start.26
  203.3 19.6 %collective-permute-start.19 = (bf16[160,1152]{1,0:T(8,128)(2,1)S(1)}, bf16[160,1152]{1,0:T(8,128)(2,1)S(1)}, u32[]{:S(2)}, u32[]{:S(2)}) collective-permute-start(bf16[160,1152]{1,0:T(8,128)(2,1)S(1)} %get-tuple-element.9), channel_id=1, source_target_pairs={{0,16},{16,0},{1,17},{17,1},{2,18},{18,2},{3,19},{19,3},{4,20},{20... | collective-permute-start | bytes 1105928 | tf_op jit(solution)/shard_map/ppermute | solution.py:16
  213.0 16.1 %collective-permute-start.27 = (bf16[160,1152]{1,0:T(8,128)(2,1)S(1)}, bf16[160,1152]{1,0:T(8,128)(2,1)S(1)}, u32[]{:S(2)}, u32[]{:S(2)}) collective-permute-start(bf16[160,1152]{1,0:T(8,128)(2,1)S(1)} %get-tuple-element.15), channel_id=1, source_target_pairs={{0,16},{16,0},{1,17},{17,1},{2,18},{18,2},{3,19},{19,3},{4,20},{20... | collective-permute-start | bytes 1105928 | tf_op jit(solution)/shard_map/ppermute | solution.py:16
  229.2 17.1 %collective-permute-start.28 = (bf16[160,1152]{1,0:T(8,128)(2,1)S(1)}, bf16[160,1152]{1,0:T(8,128)(2,1)S(1)}, u32[]{:S(2)}, u32[]{:S(2)}) collective-permute-start(bf16[160,1152]{1,0:T(8,128)(2,1)S(1)} %fusion.30), channel_id=1, source_target_pairs={{0,32},{32,0},{1,33},{33,1},{2,34},{34,2},{3,35},{35,3},{4,36},{36... | collective-permute-start | bytes 1105928 | tf_op jit(solution)/shard_map/ppermute | solution.py:16
  231.1 17.8 %collective-permute-start.21 = (bf16[160,1152]{1,0:T(8,128)(2,1)S(1)}, bf16[160,1152]{1,0:T(8,128)(2,1)S(1)}, u32[]{:S(2)}, u32[]{:S(2)}) collective-permute-start(bf16[160,1152]{1,0:T(8,128)(2,1)S(1)} %get-tuple-element.7), channel_id=1, source_target_pairs={{0,64},{64,0},{1,65},{65,1},{2,66},{66,2},{3,67},{67,3},{4,68},{68... | collective-permute-start | bytes 1105928 | tf_op jit(solution)/shard_map/ppermute | solution.py:16
  246.4 26.3 %collective-permute-start.29 = (bf16[160,1152]{1,0:T(8,128)(2,1)S(1)}, bf16[160,1152]{1,0:T(8,128)(2,1)S(1)}, u32[]{:S(2)}, u32[]{:S(2)}) collective-permute-start(bf16[160,1152]{1,0:T(8,128)(2,1)S(1)} %get-tuple-element.13), channel_id=1, source_target_pairs={{0,64},{64,0},{1,65},{65,1},{2,66},{66,2},{3,67},{67,3},{4,68},{68... | collective-permute-start | bytes 1105928 | tf_op jit(solution)/shard_map/ppermute | solution.py:16
  249.0 36.1 %collective-permute-start.22 = (bf16[160,1152]{1,0:T(8,128)(2,1)S(1)}, bf16[160,1152]{1,0:T(8,128)(2,1)S(1)}, u32[]{:S(2)}, u32[]{:S(2)}) collective-permute-start(bf16[160,1152]{1,0:T(8,128)(2,1)S(1)} %fusion.27), channel_id=1, source_target_pairs={{0,128},{128,0},{1,129},{129,1},{2,130},{130,2},{3,131},{131,3},{4... | collective-permute-start | bytes 1105928 | tf_op jit(solution)/shard_map/ppermute | solution.py:16
  272.8 27.7 %collective-permute-start.30 = (bf16[160,1152]{1,0:T(8,128)(2,1)S(1)}, bf16[160,1152]{1,0:T(8,128)(2,1)S(1)}, u32[]{:S(2)}, u32[]{:S(2)}) collective-permute-start(bf16[160,1152]{1,0:T(8,128)(2,1)S(1)} %fusion.31), channel_id=1, source_target_pairs={{0,128},{128,0},{1,129},{129,1},{2,130},{130,2},{3,131},{131,3},{4... | collective-permute-start | bytes 1105928 | tf_op jit(solution)/shard_map/ppermute | solution.py:16
  1040.5 68.8 %collective-permute-start.31 = (f32[96,128]{1,0:T(8,128)S(1)}, f32[96,128]{1,0:T(8,128)S(1)}, u32[]{:S(2)}, u32[]{:S(2)}) collective-permute-start(f32[96,128]{1,0:T(8,128)S(1)} %fusion), channel_id=1, source_target_pairs={{0,1},{1,2},{2,3},{3,4},{4,5},{5,6},{6,7},{7,8},{8,9},{9,10},{10,1... | collective-permute-start | bytes 147464
  1048.6 73.8 %collective-permute-start.32 = (f32[96,128]{1,0:T(8,128)S(1)}, f32[96,128]{1,0:T(8,128)S(1)}, u32[]{:S(2)}, u32[]{:S(2)}) collective-permute-start(f32[96,128]{1,0:T(8,128)S(1)} %fusion), channel_id=1, source_target_pairs={{0,2},{1,3},{2,4},{3,5},{4,6},{5,7},{6,8},{7,9},{8,10},{9,11},{10,... | collective-permute-start | bytes 147464
  1061.7 73.8 %collective-permute-start.33 = (f32[96,128]{1,0:T(8,128)S(1)}, f32[96,128]{1,0:T(8,128)S(1)}, u32[]{:S(2)}, u32[]{:S(2)}) collective-permute-start(f32[96,128]{1,0:T(8,128)S(1)} %fusion), channel_id=1, source_target_pairs={{0,3},{1,4},{2,5},{3,6},{4,7},{5,8},{6,9},{7,10},{8,11},{9,12},{10... | collective-permute-start | bytes 147464
  1074.9 73.8 %collective-permute-start.34 = (f32[96,128]{1,0:T(8,128)S(1)}, f32[96,128]{1,0:T(8,128)S(1)}, u32[]{:S(2)}, u32[]{:S(2)}) collective-permute-start(f32[96,128]{1,0:T(8,128)S(1)} %fusion), channel_id=1, source_target_pairs={{0,4},{1,5},{2,6},{3,7},{4,8},{5,9},{6,10},{7,11},{8,12},{9,13},{1... | collective-permute-start | bytes 147464
  1092.7 69.2 %collective-permute-start.35 = (f32[96,128]{1,0:T(8,128)S(1)}, f32[96,128]{1,0:T(8,128)S(1)}, u32[]{:S(2)}, u32[]{:S(2)}) collective-permute-start(f32[96,128]{1,0:T(8,128)S(1)} %fusion), channel_id=1, source_target_pairs={{0,5},{1,6},{2,7},{3,8},{4,9},{5,10},{6,11},{7,12},{8,13},{9,14},{... | collective-permute-start | bytes 147464
  1109.3 65.7 %collective-permute-start.36 = (f32[96,128]{1,0:T(8,128)S(1)}, f32[96,128]{1,0:T(8,128)S(1)}, u32[]{:S(2)}, u32[]{:S(2)}) collective-permute-start(f32[96,128]{1,0:T(8,128)S(1)} %fusion), channel_id=1, source_target_pairs={{0,6},{1,7},{2,8},{3,9},{4,10},{5,11},{6,12},{7,13},{8,14},{9,15},... | collective-permute-start | bytes 147464
  1122.4 65.7 %collective-permute-start.37 = (f32[96,128]{1,0:T(8,128)S(1)}, f32[96,128]{1,0:T(8,128)S(1)}, u32[]{:S(2)}, u32[]{:S(2)}) collective-permute-start(f32[96,128]{1,0:T(8,128)S(1)} %fusion), channel_id=1, source_target_pairs={{0,7},{1,8},{2,9},{3,10},{4,11},{5,12},{6,13},{7,14},{8,15},{9,16}... | collective-permute-start | bytes 147464
  1135.6 65.7 %collective-permute-start.38 = (f32[96,128]{1,0:T(8,128)S(1)}, f32[96,128]{1,0:T(8,128)S(1)}, u32[]{:S(2)}, u32[]{:S(2)}) collective-permute-start(f32[96,128]{1,0:T(8,128)S(1)} %fusion), channel_id=1, source_target_pairs={{0,8},{1,9},{2,10},{3,11},{4,12},{5,13},{6,14},{7,15},{8,16},{9,17... | collective-permute-start | bytes 147464
  1148.7 65.7 %collective-permute-start.39 = (f32[96,128]{1,0:T(8,128)S(1)}, f32[96,128]{1,0:T(8,128)S(1)}, u32[]{:S(2)}, u32[]{:S(2)}) collective-permute-start(f32[96,128]{1,0:T(8,128)S(1)} %fusion), channel_id=1, source_target_pairs={{0,9},{1,10},{2,11},{3,12},{4,13},{5,14},{6,15},{7,16},{8,17},{9,1... | collective-permute-start | bytes 147464
  1161.9 65.7 %collective-permute-start.40 = (f32[96,128]{1,0:T(8,128)S(1)}, f32[96,128]{1,0:T(8,128)S(1)}, u32[]{:S(2)}, u32[]{:S(2)}) collective-permute-start(f32[96,128]{1,0:T(8,128)S(1)} %fusion), channel_id=1, source_target_pairs={{0,10},{1,11},{2,12},{3,13},{4,14},{5,15},{6,16},{7,17},{8,18},{9,... | collective-permute-start | bytes 147464
  1175.0 65.7 %collective-permute-start.41 = (f32[96,128]{1,0:T(8,128)S(1)}, f32[96,128]{1,0:T(8,128)S(1)}, u32[]{:S(2)}, u32[]{:S(2)}) collective-permute-start(f32[96,128]{1,0:T(8,128)S(1)} %fusion), channel_id=1, source_target_pairs={{0,11},{1,12},{2,13},{3,14},{4,15},{5,16},{6,17},{7,18},{8,19},{9,... | collective-permute-start | bytes 147464
  1188.1 65.7 %collective-permute-start.42 = (f32[96,128]{1,0:T(8,128)S(1)}, f32[96,128]{1,0:T(8,128)S(1)}, u32[]{:S(2)}, u32[]{:S(2)}) collective-permute-start(f32[96,128]{1,0:T(8,128)S(1)} %fusion), channel_id=1, source_target_pairs={{0,12},{1,13},{2,14},{3,15},{4,16},{5,17},{6,18},{7,19},{8,20},{9,... | collective-permute-start | bytes 147464
  1201.3 65.7 %collective-permute-start.43 = (f32[96,128]{1,0:T(8,128)S(1)}, f32[96,128]{1,0:T(8,128)S(1)}, u32[]{:S(2)}, u32[]{:S(2)}) collective-permute-start(f32[96,128]{1,0:T(8,128)S(1)} %fusion), channel_id=1, source_target_pairs={{0,13},{1,14},{2,15},{3,16},{4,17},{5,18},{6,19},{7,20},{8,21},{9,... | collective-permute-start | bytes 147464
  1214.4 65.7 %collective-permute-start.44 = (f32[96,128]{1,0:T(8,128)S(1)}, f32[96,128]{1,0:T(8,128)S(1)}, u32[]{:S(2)}, u32[]{:S(2)}) collective-permute-start(f32[96,128]{1,0:T(8,128)S(1)} %fusion), channel_id=1, source_target_pairs={{0,14},{1,15},{2,16},{3,17},{4,18},{5,19},{6,20},{7,21},{8,22},{9,... | collective-permute-start | bytes 147464
  1227.6 65.7 %collective-permute-start.45 = (f32[96,128]{1,0:T(8,128)S(1)}, f32[96,128]{1,0:T(8,128)S(1)}, u32[]{:S(2)}, u32[]{:S(2)}) collective-permute-start(f32[96,128]{1,0:T(8,128)S(1)} %fusion), channel_id=1, source_target_pairs={{0,15},{1,16},{2,17},{3,18},{4,19},{5,20},{6,21},{7,22},{8,23},{9,... | collective-permute-start | bytes 147464
  1240.7 58.4 %collective-permute-start.46 = (f32[96,128]{1,0:T(8,128)S(1)}, f32[96,128]{1,0:T(8,128)S(1)}, u32[]{:S(2)}, u32[]{:S(2)}) collective-permute-start(f32[96,128]{1,0:T(8,128)S(1)} %fusion), channel_id=1, source_target_pairs={{0,16},{1,17},{2,18},{3,19},{4,20},{5,21},{6,22},{7,23},{8,24},{9,... | collective-permute-start | bytes 147464
  1253.8 48.3 %collective-permute-start.47 = (f32[96,128]{1,0:T(8,128)S(1)}, f32[96,128]{1,0:T(8,128)S(1)}, u32[]{:S(2)}, u32[]{:S(2)}) collective-permute-start(f32[96,128]{1,0:T(8,128)S(1)} %fusion), channel_id=1, source_target_pairs={{0,17},{1,18},{2,19},{3,20},{4,21},{5,22},{6,23},{7,24},{8,25},{9,... | collective-permute-start | bytes 147464
  1267.0 41.5 %collective-permute-start.48 = (f32[96,128]{1,0:T(8,128)S(1)}, f32[96,128]{1,0:T(8,128)S(1)}, u32[]{:S(2)}, u32[]{:S(2)}) collective-permute-start(f32[96,128]{1,0:T(8,128)S(1)} %fusion), channel_id=1, source_target_pairs={{0,18},{1,19},{2,20},{3,21},{4,22},{5,23},{6,24},{7,25},{8,26},{9,... | collective-permute-start | bytes 147464
  1280.1 32.2 %collective-permute-start.49 = (f32[96,128]{1,0:T(8,128)S(1)}, f32[96,128]{1,0:T(8,128)S(1)}, u32[]{:S(2)}, u32[]{:S(2)}) collective-permute-start(f32[96,128]{1,0:T(8,128)S(1)} %fusion), channel_id=1, source_target_pairs={{0,19},{1,20},{2,21},{3,22},{4,23},{5,24},{6,25},{7,26},{8,27},{9,... | collective-permute-start | bytes 147464
  1293.3 24.0 %collective-permute-start.50 = (f32[96,128]{1,0:T(8,128)S(1)}, f32[96,128]{1,0:T(8,128)S(1)}, u32[]{:S(2)}, u32[]{:S(2)}) collective-permute-start(f32[96,128]{1,0:T(8,128)S(1)} %fusion), channel_id=1, source_target_pairs={{0,20},{1,21},{2,22},{3,23},{4,24},{5,25},{6,26},{7,27},{8,28},{9,... | collective-permute-start | bytes 147464
  1299.1 21.2 %collective-permute-start.51 = (f32[96,128]{1,0:T(8,128)S(1)}, f32[96,128]{1,0:T(8,128)S(1)}, u32[]{:S(2)}, u32[]{:S(2)}) collective-permute-start(f32[96,128]{1,0:T(8,128)S(1)} %fusion), channel_id=1, source_target_pairs={{0,21},{1,22},{2,23},{3,24},{4,25},{5,26},{6,27},{7,28},{8,29},{9,... | collective-permute-start | bytes 147464
  1302.1 20.8 %collective-permute-start.52 = (f32[96,128]{1,0:T(8,128)S(1)}, f32[96,128]{1,0:T(8,128)S(1)}, u32[]{:S(2)}, u32[]{:S(2)}) collective-permute-start(f32[96,128]{1,0:T(8,128)S(1)} %fusion), channel_id=1, source_target_pairs={{0,22},{1,23},{2,24},{3,25},{4,26},{5,27},{6,28},{7,29},{8,30},{9,... | collective-permute-start | bytes 147464
  1308.5 19.8 %collective-permute-start.53 = (f32[96,128]{1,0:T(8,128)S(1)}, f32[96,128]{1,0:T(8,128)S(1)}, u32[]{:S(2)}, u32[]{:S(2)}) collective-permute-start(f32[96,128]{1,0:T(8,128)S(1)} %fusion), channel_id=1, source_target_pairs={{0,23},{1,24},{2,25},{3,26},{4,27},{5,28},{6,29},{7,30},{8,31},{9,... | collective-permute-start | bytes 147464
  1312.4 20.9 %collective-permute-start.54 = (f32[96,128]{1,0:T(8,128)S(1)}, f32[96,128]{1,0:T(8,128)S(1)}, u32[]{:S(2)}, u32[]{:S(2)}) collective-permute-start(f32[96,128]{1,0:T(8,128)S(1)} %fusion), channel_id=1, source_target_pairs={{0,24},{1,25},{2,26},{3,27},{4,28},{5,29},{6,30},{7,31},{8,32},{9,... | collective-permute-start | bytes 147464
  1317.2 19.3 %collective-permute-start.55 = (f32[96,128]{1,0:T(8,128)S(1)}, f32[96,128]{1,0:T(8,128)S(1)}, u32[]{:S(2)}, u32[]{:S(2)}) collective-permute-start(f32[96,128]{1,0:T(8,128)S(1)} %fusion), channel_id=1, source_target_pairs={{0,25},{1,26},{2,27},{3,28},{4,29},{5,30},{6,31},{7,32},{8,33},{9,... | collective-permute-start | bytes 147464
  1320.4 20.0 %collective-permute-start.56 = (f32[96,128]{1,0:T(8,128)S(1)}, f32[96,128]{1,0:T(8,128)S(1)}, u32[]{:S(2)}, u32[]{:S(2)}) collective-permute-start(f32[96,128]{1,0:T(8,128)S(1)} %fusion), channel_id=1, source_target_pairs={{0,26},{1,27},{2,28},{3,29},{4,30},{5,31},{6,32},{7,33},{8,34},{9,... | collective-permute-start | bytes 147464
  1322.9 19.1 %collective-permute-start.57 = (f32[96,128]{1,0:T(8,128)S(1)}, f32[96,128]{1,0:T(8,128)S(1)}, u32[]{:S(2)}, u32[]{:S(2)}) collective-permute-start(f32[96,128]{1,0:T(8,128)S(1)} %fusion), channel_id=1, source_target_pairs={{0,27},{1,28},{2,29},{3,30},{4,31},{5,32},{6,33},{7,34},{8,35},{9,... | collective-permute-start | bytes 147464
  1328.3 15.0 %collective-permute-start.58 = (f32[96,128]{1,0:T(8,128)S(1)}, f32[96,128]{1,0:T(8,128)S(1)}, u32[]{:S(2)}, u32[]{:S(2)}) collective-permute-start(f32[96,128]{1,0:T(8,128)S(1)} %fusion), channel_id=1, source_target_pairs={{0,28},{1,29},{2,30},{3,31},{4,32},{5,33},{6,34},{7,35},{8,36},{9,... | collective-permute-start | bytes 147464
  1333.3 11.3 collective-permute-start.59
  1336.5 10.4 collective-permute-start.60
  1342.0 10.4 collective-permute-start.62
  1343.3 11.9 collective-permute-start.63
  1344.7 12.5 collective-permute-start.64
  1347.0 12.2 collective-permute-start.65
  1348.9 10.3 collective-permute-start.66
  (30 other events, 1618.8 us)
where the time goes:
time: 1430 us; the launch traced here: 1420 us
  blocking collectives  710 us (50%)
  starting transfers between devices  428 us (30%)
  waiting for transfers between devices  170 us (12%)
  local copies, waits for them, and re-layouts  85.3 us (6%)
    unnamed x1, blocking collectives  710 us
    unnamed x40, starting transfers between devices  317 us
    ppermute x31, waiting for transfers between devices, from_partner(): return lax.ppermute(block, axis, route)  168 us
    ppermute x31, starting transfers between devices, from_partner(): return lax.ppermute(block, axis, route)  111 us
    unnamed x49, local copies, waits for them, and re-layouts  60.6 us
  transfers between devices with their start and end apart: 71, of which 27 were waited for; matrix products, arithmetic and copies ran while one was open for 1% of the time, Pallas kernels for 0%

commit v1 on v0

v1 whole, which is shorter than its diff:
```python
import jax
import jax.numpy as jnp
from jax import lax
from jax.experimental import pallas as pl
from jax.experimental.pallas import tpu as pltpu
from jax.sharding import PartitionSpec as P

EPS = 1e-06
AXIS = "dp"
NZ, NX, NY, NCORE = 8, 4, 4, 2
BF = jnp.bfloat16
F32 = jnp.float32
ROWS, WIDTH = 160, 1152
HALF = WIDTH // 2
GROUP = 36
BLOCK = 4 * GROUP
CUTS = ((0, 640), (640, 1152))


def swap(x, flip):
    if flip == 0:
        return x
    return lax.ppermute(x, AXIS, [(i, i ^ flip) for i in range(NZ * NX * NY * NCORE)])


def code(z=0, x=0, y=0, core=0):
    return ((z * NX + x) * NY + y) * NCORE + core


def exchange(feat, masks):
    z = masks // (NX * NY * NCORE)
    xy = masks // NCORE % (NX * NY)
    branches = [
        lambda a, b, p=p, q=q: (swap(a, code(z=p)), swap(b, code(x=q // NY, y=q % NY)))
        for p in range(NZ) for q in range(NX * NY)
    ]

    def leg(at, pair):
        ahead, behind = pair
        ahead, behind = lax.switch(z[at] * 16 + xy[1 - at], branches, ahead, behind)
        return behind, ahead

    return lax.fori_loop(0, 2, leg, (feat, feat))


def dot(a, b, ca=1, cb=0):
    return lax.dot_general(a, b, (((ca,), (cb,)), ((), ())), preferred_element_type=F32)


def normalize(y):
    r = lax.rsqrt(jnp.sum(y * y, axis=-1, keepdims=True) + EPS)
    return y * r, r


def backnorm(dz, z, r):
    return r * (dz - z * jnp.sum(z * dz, axis=-1, keepdims=True))


def row_order():
    me = lax.axis_index(AXIS)
    pos = lax.broadcasted_iota(jnp.int32, (HALF, 1), 0)
    ninth = (pos * 7282) >> 16
    row = pos - 9 * ninth
    z = (ninth & 3) ^ ((me >> 5) & 3)
    x = ((ninth >> 2) & 3) ^ ((me >> 3) & 3)
    y = ((ninth >> 4) & 3) ^ ((me >> 1) & 3)
    src = (((z * 4 + x) * 4 + y) * 2 + (me & 1)) * 9 + row
    feature = lax.broadcasted_iota(jnp.int32, (HALF, WIDTH), 1)
    return jnp.where(feature == src, 1.0, 0.0).astype(BF)


def pick(masks_ref, index, same, other):
    odd = (masks_ref[index] & 1) == 1
    same, other = same[...], other[...]
    return jnp.where(odd, other, same), jnp.where(odd, same, other)


def local_kernel(img_ref, own_ref, same0, same1, other0, other1, ihead_ref, thead_ref,
                 ls_ref, lb_ref, masks_ref, dy_ref):
    first, _ = pick(masks_ref, 0, same0, other0)
    second, _ = pick(masks_ref, 1, same1, other1)
    txt = jnp.concatenate([own_ref[...], first, second], axis=0)
    zi, ri = normalize(dot(img_ref[...], ihead_ref[...]))
    zt, rt = normalize(dot(txt, thead_ref[...]))
    zib = zi.astype(BF)
    ztb = zt.astype(BF)
    scale = jnp.exp(jnp.full((1, 1), ls_ref[0], F32))
    logits = scale * dot(zib, ztb, 1, 1) + lb_ref[0]
    here = lax.broadcasted_iota(jnp.int32, logits.shape, 0) == lax.broadcasted_iota(jnp.int32, logits.shape, 1)
    diff = 1.0 / (1.0 + jnp.exp(-logits)) - jnp.where(here, 1.0, 0.0)
    g = diff / 16.0
    dy_ref[:ROWS, :] = backnorm(scale * dot(g.astype(BF), ztb), zi, ri).astype(BF)
    dy_ref[ROWS:, :] = backnorm(scale * dot(g.T.astype(BF), zib), zt, rt).astype(BF)


def deal_kernel(img_ref, img2_ref, own_ref, own2_ref, same0, same1, other0, other1,
                masks_ref, dimg_ref, dtxt_ref):
    order = row_order()
    first, first2 = pick(masks_ref, 0, same0, other0)
    second, second2 = pick(masks_ref, 1, same1, other1)
    img = jnp.concatenate([img_ref[...], img2_ref[...]], axis=0)
    txt = jnp.concatenate([own_ref[...], first, second, own2_ref[...], first2, second2], axis=0)
    dimg_ref[...] = dot(order, img, 1, 1).astype(BF)
    dtxt_ref[...] = dot(order, txt, 1, 1).astype(BF)


def gradient_kernel(dimg_ref, dtxt_ref, dy_ref, dy2_ref, *outs):
    sides = ((dimg_ref, slice(0, ROWS)), (dtxt_ref, slice(ROWS, 4 * ROWS)))
    for part, (low, high) in enumerate(CUTS):
        wide = high - low
        for side, (dealt_ref, rows) in enumerate(sides):
            dy = jnp.concatenate([dy_ref[rows, low:high], dy2_ref[rows, low:high]], axis=0)
            grad = dot(dealt_ref[...], dy)
            to = slice(side * wide, (side + 1) * wide)
            for d in range(4):
                if part == 0:
                    block = grad[d * BLOCK:(d + 1) * BLOCK]
                else:
                    at = [(y * 4 + d) * GROUP for y in range(4)]
                    block = jnp.concatenate([grad[i:i + GROUP] for i in at], axis=0)
                ref = outs[part * 4 + d]
                ref[:, to] = block.astype(ref.dtype)


def call(kernel, outs, args, scalars, flops):
    bytes_of = lambda xs: sum(x.size * x.dtype.itemsize for x in xs)
    vmem = pl.BlockSpec(memory_space=pltpu.VMEM)
    smem = pl.BlockSpec(memory_space=pltpu.SMEM)
    return pl.pallas_call(
        kernel,
        out_shape=outs,
        in_specs=[vmem] * (len(args) - scalars) + [smem] * scalars,
        out_specs=[vmem] * len(outs),
        compiler_params=pltpu.CompilerParams(vmem_limit_bytes=56 * 2**20),
        cost_estimate=pl.CostEstimate(
            flops=flops, transcendentals=0, bytes_accessed=bytes_of(args) + bytes_of(outs)),
    )(*args)


def shape(rows, cols, kind):
    return jax.ShapeDtypeStruct((rows, cols), kind)


def spread(own, sends, flips):
    got = [[None] * 3, [None] * 3]
    for d in (1, 0, 2):
        for part in (1, 0):
            got[part][d] = swap(sends[part][d], flips[part][d])
    got = lax.optimization_barrier(got)
    return [
        own[part] + got[part][0].astype(F32) + got[part][1].astype(F32) + got[part][2].astype(F32)
        for part in range(2)
    ]


def shards(img_feat, txt_feat, img_head, txt_head, log_scale, logit_bias, masks):
    sibling = code(core=1)
    img2, txt2 = swap(img_feat, sibling), swap(txt_feat, sibling)
    same = exchange(txt_feat, masks)
    img2, txt2, same = lax.optimization_barrier((img2, txt2, same))
    others = [swap(x, sibling) for x in same]
    dy, = call(
        local_kernel, [shape(4 * ROWS, WIDTH, BF)],
        [img_feat, txt_feat, *same, *others, img_head, txt_head, log_scale, logit_bias, masks],
        3, 3 * 10**9)
    dy2 = swap(dy, sibling)
    dealt = call(
        deal_kernel, [shape(HALF, 2 * ROWS, BF), shape(HALF, 6 * ROWS, BF)],
        [img_feat, img2, txt_feat, txt2, *same, *others, masks], 1, 2 * 10**9)
    blocks = call(
        gradient_kernel,
        [shape(BLOCK, 2 * (high - low), F32 if d == 0 else BF) for low, high in CUTS for d in range(4)],
        [*dealt, dy, dy2], 0, 2 * 10**9)

    along_y = [code(y=d) for d in (1, 2, 3)]
    along_x = [code(x=d) for d in (1, 2, 3)]
    sums = spread(
        (blocks[0], blocks[4]), (blocks[1:4], blocks[5:8]), (along_y, along_x))
    rows = [slice(d * GROUP, (d + 1) * GROUP) for d in range(4)]
    sums = spread(
        [s[rows[0]] for s in sums],
        [[s[rows[d]].astype(BF) for d in (1, 2, 3)] for s in sums],
        (along_x, along_y))

    img, txt = (
        jnp.concatenate([s[:, side * (s.shape[1] // 2):(side + 1) * (s.shape[1] // 2)] for s in sums], axis=1)
        for side in range(2)
    )
    high = lax.axis_index(AXIS) >= code(z=4)
    near, far = jnp.where(high, txt, img), jnp.where(high, img, txt)
    total = near[:9]
    for d in range(1, 8):
        rows = (far if d >= 4 else near)[(d & 3) * 9:(d & 3) * 9 + 9]
        total = total + swap(rows.astype(BF), code(z=d)).astype(F32)
    return total.reshape(81, 128)


def solution(mesh):
    return jax.shard_map(
        shards,
        mesh=mesh,
        in_specs=(P("dp", None), P("dp", None), P(), P(), P(), P(), P()),
        out_specs=P("dp", None),
        check_vma=False,
    )
```

time: 1430 us -> 229 us (0.16)
  blocking collectives: 710 us -> 0 us
  starting transfers between devices: 428 us -> 50 us
  waiting for transfers between devices: 170 us -> 43.9 us
  loops' own time: 0 us -> 101 us
  local copies, waits for them, and re-layouts: 85.3 us -> 7.91 us
  Pallas kernels: 0 us -> 19.4 us
    unnamed x1 -> x0, blocking collectives: 710 us -> none
    unnamed x40 -> x0, starting transfers between devices: 317 us -> none
    ppermute x31 -> x28, waiting for transfers between devices: 168 us -> 43.9 us  [swap(): lax.ppermute(x, AXIS, [(i, i ^ flip) for i in range(NZ * NX * NY * NCORE)])]
    another operation x0 -> x3, loops' own time: none -> 101 us  [the longest x2 70.5 us: leg(): ahead, behind = lax.switch(z[at] * 16 + xy[1 - at], branches, ahead, behind)]
    ppermute x31 -> x28, starting transfers between devices: 111 us -> 50 us  [swap(): lax.ppermute(x, AXIS, [(i, i ^ flip) for i in range(NZ * NX * NY * NCORE)])]
    unnamed x49 -> x12, local copies, waits for them, and re-layouts: 60.6 us -> 4.21 us
    pallas_call x0 -> x3, Pallas kernels: none -> 19.4 us  [call(): pl.pallas_call(kernel, out_shape=outs, in_specs=[vmem] * (len(args) - sca...]
  transfers between devices with their start and end apart: 71 -> 28, of which waited for: 27 -> 12; matrix products, arithmetic and copies ran while one was open for 1% -> 2% of each run, Pallas kernels for 0% -> 2%
where the time goes in v1:
time: 229 us; the launch traced here: 225 us
  loops' own time  101 us (44%)
  starting transfers between devices  50 us (22%)
  waiting for transfers between devices  43.9 us (19%)
  Pallas kernels  19.4 us (8%)
  local copies, waits for them, and re-layouts  7.91 us (3%)
    another operation x2, loops' own time, leg(): ahead, behind = lax.switch(z[at] * 16 + xy[1 - at], branches, ahead, behind)  70.5 us
    ppermute x28, starting transfers between devices, swap(): lax.ppermute(x, AXIS, [(i, i ^ flip) for i in range(NZ * NX * NY * NCORE)])  50 us
    ppermute x28, waiting for transfers between devices, swap(): lax.ppermute(x, AXIS, [(i, i ^ flip) for i in range(NZ * NX * NY * NCORE)])  43.9 us
    another operation x1, loops' own time, exchange(): return lax.fori_loop(0, 2, leg, (feat, feat))  30.3 us
    pallas_call x3, Pallas kernels, call(): pl.pallas_call(kernel, out_shape=outs, in_specs=[vmem] * (len(args) - sca...  19.4 us
  transfers between devices with their start and end apart: 28, of which 12 were waited for; matrix products, arithmetic and copies ran while one was open for 2% of the time, Pallas kernels for 2%

profile of v1, /device:TPU:0, one launch (start us, length us, event | category | flops | bytes accessed | tf_op | source)
XLA Modules:
  0.0 225.5 jit_solution(16196254550525773446)
XLA Ops:
  0.0 0.5 collective-permute-start.233
  0.5 1.0 copy.265
  1.5 1.0 copy.266
  2.5 139.4 %while.17 = (s32[]{:T(128)}, bf16[160,1152]{1,0:T(8,128)(2,1)S(1)}, bf16[160,1152]{1,0:T(8,128)(2,1)S(1)}, s32[2]{0:T(128)S(1)}, s32[2]{0:T(128)S(1)}, /*index=5...) while((s32[]{:T(128)}, bf16[160,1152]{1,0:T(8,128)(2,1)S(1)}, ...), condition=%wide.region_129.130_spmd, body=%wide.region_0.129_spmd.sunk | while | flops 9 | bytes 6635875 | solution.py:43
  3.1 0.7 dynamic_slice.23
  3.7 0.6 dynamic_slice.22
  5.7 49.3 %conditional.2 = ((bf16[160,1152]{1,0:T(8,128)(2,1)S(1)}, bf16[160,1152]{1,0:T(8,128)(2,1)S(1)})) conditional(s32[]{:T(128)} %bitcast.2, (bf16[160,1152]{1,0:T(8,128)(2,1)S(1)}, bf16[160,1152]{1,0:T(8,128)(2,1)S(1)}) %tuple.570, (bf16[160,1152]{1,0:T(8,128)(2,1)S(1)}, bf16[160,1152]{1,0:T(8,128)(2,1)S(1)}) %tuple.571, ...), branch_computations={%region_1.1_spmd, %region_2.2_spmd, %region_3.3_spmd, %region_4.4_... | conditional | bytes 4423784 | solution.py:40
  33.3 3.0 %collective-permute-start.106 = (bf16[160,1152]{1,0:T(8,128)(2,1)S(1)}, bf16[160,1152]{1,0:T(8,128)(2,1)S(1)}, u32[]{:S(2)}, u32[]{:S(2)}) collective-permute-start(bf16[160,1152]{1,0:T(8,128)(2,1)S(1)} %get-tuple-element.776), channel_id=1, source_target_pairs={{0,96},{1,97},{2,98},{3,99},{4,100},{5,101},{6,102},{7,103},{8,104... | collective-permute-start | bytes 1105928 | tf_op jit(solution)/shard_map/while/body/eval_jaxpr/cond/branch_63_fun/ppermute | solution.py:23
  36.2 5.2 %collective-permute-start.107 = (bf16[160,1152]{1,0:T(8,128)(2,1)S(1)}, bf16[160,1152]{1,0:T(8,128)(2,1)S(1)}, u32[]{:S(2)}, u32[]{:S(2)}) collective-permute-start(bf16[160,1152]{1,0:T(8,128)(2,1)S(1)} %get-tuple-element.777), channel_id=1, source_target_pairs={{0,30},{1,31},{2,28},{3,29},{4,26},{5,27},{6,24},{7,25},{8,22},{9,... | collective-permute-start | bytes 1105928 | tf_op jit(solution)/shard_map/while/body/eval_jaxpr/cond/branch_63_fun/ppermute | solution.py:23
  41.5 4.3 %collective-permute-done.106 = bf16[160,1152]{1,0:T(8,128)(2,1)S(1)} collective-permute-done((bf16[160,1152]{1,0:T(8,128)(2,1)S(1)}, bf16[160,1152]{1,0:T(8,128)(2,1)S(1)}, u32[]{:S(2)}, u32[]{:S(2)}) %collective-permute-start.106) | collective-permute-done | bytes 368672 | tf_op jit(solution)/shard_map/while/body/eval_jaxpr/cond/branch_63_fun/ppermute | solution.py:23
  45.8 4.2 %collective-permute-done.107 = bf16[160,1152]{1,0:T(8,128)(2,1)S(1)} collective-permute-done((bf16[160,1152]{1,0:T(8,128)(2,1)S(1)}, bf16[160,1152]{1,0:T(8,128)(2,1)S(1)}, u32[]{:S(2)}, u32[]{:S(2)}) %collective-permute-start.107) | collective-permute-done | bytes 368672 | tf_op jit(solution)/shard_map/while/body/eval_jaxpr/cond/branch_63_fun/ppermute | solution.py:23
  64.4 0.7 dynamic_slice.23
  65.1 0.6 dynamic_slice.22
  67.1 57.0 %conditional.2 = ((bf16[160,1152]{1,0:T(8,128)(2,1)S(1)}, bf16[160,1152]{1,0:T(8,128)(2,1)S(1)})) conditional(s32[]{:T(128)} %bitcast.2, (bf16[160,1152]{1,0:T(8,128)(2,1)S(1)}, bf16[160,1152]{1,0:T(8,128)(2,1)S(1)}) %tuple.570, (bf16[160,1152]{1,0:T(8,128)(2,1)S(1)}, bf16[160,1152]{1,0:T(8,128)(2,1)S(1)}) %tuple.571, ...), branch_computations={%region_1.1_spmd, %region_2.2_spmd, %region_3.3_spmd, %region_4.4_... | conditional | bytes 4423784 | solution.py:40
  103.9 3.2 %collective-permute-start.206 = (bf16[160,1152]{1,0:T(8,128)(2,1)S(1)}, bf16[160,1152]{1,0:T(8,128)(2,1)S(1)}, u32[]{:S(2)}, u32[]{:S(2)}) collective-permute-start(bf16[160,1152]{1,0:T(8,128)(2,1)S(1)} %get-tuple-element.880), channel_id=1, source_target_pairs={{0,224},{1,225},{2,226},{3,227},{4,228},{5,229},{6,230},{7,231},{8... | collective-permute-start | bytes 1105928 | tf_op jit(solution)/shard_map/while/body/eval_jaxpr/cond/branch_115_fun/ppermute | solution.py:23
  107.1 2.9 %collective-permute-start.207 = (bf16[160,1152]{1,0:T(8,128)(2,1)S(1)}, bf16[160,1152]{1,0:T(8,128)(2,1)S(1)}, u32[]{:S(2)}, u32[]{:S(2)}) collective-permute-start(bf16[160,1152]{1,0:T(8,128)(2,1)S(1)} %get-tuple-element.881), channel_id=1, source_target_pairs={{0,6},{1,7},{2,4},{3,5},{4,2},{5,3},{6,0},{7,1},{8,14},{9,15},{10,... | collective-permute-start | bytes 1105928 | tf_op jit(solution)/shard_map/while/body/eval_jaxpr/cond/branch_115_fun/ppermute | solution.py:23
  110.0 12.9 %collective-permute-done.206 = bf16[160,1152]{1,0:T(8,128)(2,1)S(1)} collective-permute-done((bf16[160,1152]{1,0:T(8,128)(2,1)S(1)}, bf16[160,1152]{1,0:T(8,128)(2,1)S(1)}, u32[]{:S(2)}, u32[]{:S(2)}) %collective-permute-start.206) | collective-permute-done | bytes 368672 | tf_op jit(solution)/shard_map/while/body/eval_jaxpr/cond/branch_115_fun/ppermute | solution.py:23
  122.9 0.0 collective-permute-done.207
  141.9 0.0 collective-permute-done.232.img2_ref
  142.0 0.1 collective-permute-start.234
  142.1 0.5 collective-permute-start.235
  143.9 0.4 collective-permute-done.235.other1
  144.3 0.3 copy-done.2
  144.6 0.7 copy-done.3
  145.3 8.5 %shard_map.74.dy_ref = bf16[640,1152]{1,0:T(8,128)(2,1)} custom-call(bf16[160,1152]{1,0:T(8,128)(2,1)} %img_ref.3, bf16[160,1152]{1,0:T(8,128)(2,1)} %own_ref.3, bf16[160,1152]{1,0:T(8,128)(2,1)S(1)} %get-tuple-element.946.same0, bf16[160,1152]{1,0:T(8,128)(2,1)S(1)} %get-tuple-element.947.same1, bf16[160,1152]{1,0:T(8,128)(2,1)} %copy-done.2, ...), custom_call_target="tpu_custom_call" | custom-call | flops 3000000000 | bytes 8994832 | tf_op jit(solution)/shard_map/pallas_call | solution.py:129
  153.8 0.1 collective-permute-start.236
  154.0 5.2 %shard_map.73 = (bf16[576,320]{1,0:T(8,128)(2,1)}, bf16[576,960]{1,0:T(8,128)(2,1)}) custom-call(bf16[160,1152]{1,0:T(8,128)(2,1)} %img_ref.3, bf16[160,1152]{1,0:T(8,128)(2,1)} %collective-permute-done.232.img2_ref, bf16[160,1152]{1,0:T(8,128)(2,1)} %own_ref.3, bf16[160,1152]{1,0:T(8,128)(2,1)} %collective-permute-done.233.own2_ref, ...), custom_call_target="tpu_custom_call" | custom-call | flops 2000000000 | bytes 4423688 | tf_op jit(solution)/shard_map/pallas_call | solution.py:129
  159.1 0.0 collective-permute-done.236.dy2_ref
  159.1 1.1 copy-done.1
  160.3 5.8 %shard_map.75 = (f32[144,1280]{1,0:T(8,128)}, bf16[144,1280]{1,0:T(8,128)(2,1)}, bf16[144,1280]{1,0:T(8,128)(2,1)}, bf16[144,1280]{1,0:T(8,128)(2,1)}, f32[144,1...) custom-call(bf16[576,320]{1,0:T(8,128)(2,1)} %get-tuple-element.948.dimg_ref, ...), custom_call_target="tpu_custom_call" | custom-call | flops 2000000000 | bytes 7741440 | tf_op jit(solution)/shard_map/pallas_call | solution.py:129
  166.0 0.2 collective-permute-start.240
  166.2 0.2 collective-permute-start.237
  166.4 4.1 %collective-permute-start.238 = (bf16[144,1280]{1,0:T(8,128)(2,1)}, bf16[144,1280]{1,0:T(8,128)(2,1)S(1)}, u32[]{:S(2)}, u32[]{:S(2)}) collective-permute-start(bf16[144,1280]{1,0:T(8,128)(2,1)} %get-tuple-element.952), channel_id=1, source_target_pairs={{0,4},{1,5},{2,6},{3,7},{4,0},{5,1},{6,2},{7,3},{8,12},{9,13},{10,... | collective-permute-start | bytes 1105928 | tf_op jit(solution)/shard_map/ppermute | solution.py:23
  170.5 0.4 collective-permute-start.239
  170.9 3.8 %collective-permute-start.241 = (bf16[144,1024]{1,0:T(8,128)(2,1)}, bf16[144,1024]{1,0:T(8,128)(2,1)S(1)}, u32[]{:S(2)}, u32[]{:S(2)}) collective-permute-start(bf16[144,1024]{1,0:T(8,128)(2,1)} %get-tuple-element.955), channel_id=1, source_target_pairs={{0,16},{1,17},{2,18},{3,19},{4,20},{5,21},{6,22},{7,23},{8,24},{9,... | collective-permute-start | bytes 884744 | tf_op jit(solution)/shard_map/ppermute | solution.py:23
  174.7 1.4 collective-permute-done.240
  176.1 2.6 %collective-permute-start.242 = (bf16[144,1024]{1,0:T(8,128)(2,1)}, bf16[144,1024]{1,0:T(8,128)(2,1)S(1)}, u32[]{:S(2)}, u32[]{:S(2)}) collective-permute-start(bf16[144,1024]{1,0:T(8,128)(2,1)} %get-tuple-element.956), channel_id=1, source_target_pairs={{0,24},{1,25},{2,26},{3,27},{4,28},{5,29},{6,30},{7,31},{8,16},{9,... | collective-permute-start | bytes 884744 | tf_op jit(solution)/shard_map/ppermute | solution.py:23
  178.7 5.2 %collective-permute-done.241 = bf16[144,1024]{1,0:T(8,128)(2,1)S(1)} collective-permute-done((bf16[144,1024]{1,0:T(8,128)(2,1)}, bf16[144,1024]{1,0:T(8,128)(2,1)S(1)}, u32[]{:S(2)}, u32[]{:S(2)}) %collective-permute-start.241) | collective-permute-done | bytes 294944 | tf_op jit(solution)/shard_map/ppermute | solution.py:23
  183.9 6.2 %collective-permute-done.242 = bf16[144,1024]{1,0:T(8,128)(2,1)S(1)} collective-permute-done((bf16[144,1024]{1,0:T(8,128)(2,1)}, bf16[144,1024]{1,0:T(8,128)(2,1)S(1)}, u32[]{:S(2)}, u32[]{:S(2)}) %collective-permute-start.242) | collective-permute-done | bytes 294944 | tf_op jit(solution)/shard_map/ppermute | solution.py:23
  190.1 0.0 collective-permute-done.237
  190.1 0.0 collective-permute-done.238
  190.1 1.2 fusion.14
  191.4 0.5 collective-permute-start.246
  191.9 0.2 fusion.15
  192.1 0.1 fusion.16
  192.1 1.3 collective-permute-start.243
  193.4 2.6 %collective-permute-start.244 = (bf16[36,1280]{1,0:T(8,128)(2,1)S(1)}, bf16[36,1280]{1,0:T(8,128)(2,1)S(1)}, u32[]{:S(2)}, u32[]{:S(2)}) collective-permute-start(bf16[36,1280]{1,0:T(8,128)(2,1)S(1)} %get-tuple-element.987), channel_id=1, source_target_pairs={{0,16},{1,17},{2,18},{3,19},{4,20},{5,21},{6,22},{7,23},{8,24},{9,... | collective-permute-start | bytes 276488 | tf_op jit(solution)/shard_map/ppermute | solution.py:23
  196.0 1.0 collective-permute-start.245
  196.9 4.1 %collective-permute-start.247 = (bf16[36,1024]{1,0:T(8,128)(2,1)S(1)}, bf16[36,1024]{1,0:T(8,128)(2,1)S(1)}, u32[]{:S(2)}, u32[]{:S(2)}) collective-permute-start(bf16[36,1024]{1,0:T(8,128)(2,1)S(1)} %get-tuple-element.990), channel_id=1, source_target_pairs={{0,4},{1,5},{2,6},{3,7},{4,0},{5,1},{6,2},{7,3},{8,12},{9,13},{10,... | collective-permute-start | bytes 221192 | tf_op jit(solution)/shard_map/ppermute | solution.py:23
  201.0 0.2 collective-permute-start.248
  201.3 2.2 collective-permute-done.247
  203.5 3.2 %collective-permute-done.248 = bf16[36,1024]{1,0:T(8,128)(2,1)S(1)} collective-permute-done((bf16[36,1024]{1,0:T(8,128)(2,1)S(1)}, bf16[36,1024]{1,0:T(8,128)(2,1)S(1)}, u32[]{:S(2)}, u32[]{:S(2)}) %collective-permute-start.248) | collective-permute-done | bytes 73760 | tf_op jit(solution)/shard_map/ppermute | solution.py:23
  206.7 0.1 fusion.1
  207.0 4.4 %collective-permute-start.252 = (bf16[9,1152]{1,0:T(8,128)(2,1)S(1)}, bf16[9,1152]{1,0:T(8,128)(2,1)S(1)}, u32[]{:S(2)}, u32[]{:S(2)}) collective-permute-start(bf16[9,1152]{1,0:T(8,128)(2,1)S(1)} %get-tuple-element.999), channel_id=1, source_target_pairs={{0,128},{1,129},{2,130},{3,131},{4,132},{5,133},{6,134},{7,135},{8... | collective-permute-start | bytes 62216 | tf_op jit(solution)/shard_map/ppermute | solution.py:23
  211.4 0.1 collective-permute-start.253
  211.5 4.5 %collective-permute-start.254 = (bf16[9,1152]{1,0:T(8,128)(2,1)S(1)}, bf16[9,1152]{1,0:T(8,128)(2,1)S(1)}, u32[]{:S(2)}, u32[]{:S(2)}) collective-permute-start(bf16[9,1152]{1,0:T(8,128)(2,1)S(1)} %get-tuple-element.1001), channel_id=1, source_target_pairs={{0,192},{1,193},{2,194},{3,195},{4,196},{5,197},{6,198},{7,199},{8... | collective-permute-start | bytes 62216 | tf_op jit(solution)/shard_map/ppermute | solution.py:23
  215.9 0.3 collective-permute-start.255
  216.2 1.3 collective-permute-start.249
  217.5 1.3 collective-permute-start.250
  218.8 1.9 collective-permute-start.251
  220.7 0.4 collective-permute-done.255
  221.1 1.7 collective-permute-done.250
  222.8 1.8 collective-permute-done.251
  224.6 0.6 reshape.9
  (39 shorter events, 0.6 us)
Async XLA Ops:
  0.0 2.5 %copy-start.4 = (s32[2]{0:T(128)S(1)}, s32[2]{0:T(128)}, u32[]{:S(2)}) copy-start(s32[2]{0:T(128)} %masks_ref.3) | copy-start | bytes 28
  0.0 141.9 %collective-permute-start.232 = (bf16[160,1152]{1,0:T(8,128)(2,1)}, bf16[160,1152]{1,0:T(8,128)(2,1)}, u32[]{:S(2)}, u32[]{:S(2)}) collective-permute-start(bf16[160,1152]{1,0:T(8,128)(2,1)} %img_ref.3), channel_id=1, source_target_pairs={{0,1},{1,0},{2,3},{3,2},{4,5},{5,4},{6,7},{7,6},{8,9},{9,8},{10,11... | collective-permute-start | bytes 1105928 | tf_op jit(solution)/shard_map/ppermute | solution.py:23
  0.0 141.9 %collective-permute-start.233 = (bf16[160,1152]{1,0:T(8,128)(2,1)}, bf16[160,1152]{1,0:T(8,128)(2,1)}, u32[]{:S(2)}, u32[]{:S(2)}) collective-permute-start(bf16[160,1152]{1,0:T(8,128)(2,1)} %own_ref.3), channel_id=1, source_target_pairs={{0,1},{1,0},{2,3},{3,2},{4,5},{5,4},{6,7},{7,6},{8,9},{9,8},{10,11... | collective-permute-start | bytes 1105928 | tf_op jit(solution)/shard_map/ppermute | solution.py:23
  33.3 12.5 %collective-permute-start.106 = (bf16[160,1152]{1,0:T(8,128)(2,1)S(1)}, bf16[160,1152]{1,0:T(8,128)(2,1)S(1)}, u32[]{:S(2)}, u32[]{:S(2)}) collective-permute-start(bf16[160,1152]{1,0:T(8,128)(2,1)S(1)} %get-tuple-element.776), channel_id=1, source_target_pairs={{0,96},{1,97},{2,98},{3,99},{4,100},{5,101},{6,102},{7,103},{8,104... | collective-permute-start | bytes 1105928 | tf_op jit(solution)/shard_map/while/body/eval_jaxpr/cond/branch_63_fun/ppermute | solution.py:23
  36.2 13.8 %collective-permute-start.107 = (bf16[160,1152]{1,0:T(8,128)(2,1)S(1)}, bf16[160,1152]{1,0:T(8,128)(2,1)S(1)}, u32[]{:S(2)}, u32[]{:S(2)}) collective-permute-start(bf16[160,1152]{1,0:T(8,128)(2,1)S(1)} %get-tuple-element.777), channel_id=1, source_target_pairs={{0,30},{1,31},{2,28},{3,29},{4,26},{5,27},{6,24},{7,25},{8,22},{9,... | collective-permute-start | bytes 1105928 | tf_op jit(solution)/shard_map/while/body/eval_jaxpr/cond/branch_63_fun/ppermute | solution.py:23
  103.9 19.0 %collective-permute-start.206 = (bf16[160,1152]{1,0:T(8,128)(2,1)S(1)}, bf16[160,1152]{1,0:T(8,128)(2,1)S(1)}, u32[]{:S(2)}, u32[]{:S(2)}) collective-permute-start(bf16[160,1152]{1,0:T(8,128)(2,1)S(1)} %get-tuple-element.880), channel_id=1, source_target_pairs={{0,224},{1,225},{2,226},{3,227},{4,228},{5,229},{6,230},{7,231},{8... | collective-permute-start | bytes 1105928 | tf_op jit(solution)/shard_map/while/body/eval_jaxpr/cond/branch_115_fun/ppermute | solution.py:23
  107.1 15.8 %collective-permute-start.207 = (bf16[160,1152]{1,0:T(8,128)(2,1)S(1)}, bf16[160,1152]{1,0:T(8,128)(2,1)S(1)}, u32[]{:S(2)}, u32[]{:S(2)}) collective-permute-start(bf16[160,1152]{1,0:T(8,128)(2,1)S(1)} %get-tuple-element.881), channel_id=1, source_target_pairs={{0,6},{1,7},{2,4},{3,5},{4,2},{5,3},{6,0},{7,1},{8,14},{9,15},{10,... | collective-permute-start | bytes 1105928 | tf_op jit(solution)/shard_map/while/body/eval_jaxpr/cond/branch_115_fun/ppermute | solution.py:23
  142.0 1.9 collective-permute-start.234
  142.1 2.2 collective-permute-start.235
  143.9 0.7 copy-start.2
  144.6 0.7 copy-start.3
  153.8 5.3 %collective-permute-start.236 = (bf16[640,1152]{1,0:T(8,128)(2,1)}, bf16[640,1152]{1,0:T(8,128)(2,1)S(1)}, u32[]{:S(2)}, u32[]{:S(2)}) collective-permute-start(bf16[640,1152]{1,0:T(8,128)(2,1)} %shard_map.74.dy_ref), channel_id=1, source_target_pairs={{0,1},{1,0},{2,3},{3,2},{4,5},{5,4},{6,7},{7,6},{8,9},{9,8},{10,11... | collective-permute-start | bytes 4423688 | tf_op jit(solution)/shard_map/ppermute | solution.py:23
  159.1 1.2 copy-start.1
  166.0 25.9 %copy-start = (f32[144,1280]{1,0:T(8,128)S(1)}, f32[144,1280]{1,0:T(8,128)}, u32[]{:S(2)}) copy-start(f32[144,1280]{1,0:T(8,128)} %get-tuple-element.950) | copy-start | bytes 2211844
  166.0 10.0 %collective-permute-start.240 = (bf16[144,1024]{1,0:T(8,128)(2,1)}, bf16[144,1024]{1,0:T(8,128)(2,1)S(1)}, u32[]{:S(2)}, u32[]{:S(2)}) collective-permute-start(bf16[144,1024]{1,0:T(8,128)(2,1)} %get-tuple-element.954), channel_id=1, source_target_pairs={{0,8},{1,9},{2,10},{3,11},{4,12},{5,13},{6,14},{7,15},{8,0},{9,1},... | collective-permute-start | bytes 884744 | tf_op jit(solution)/shard_map/ppermute | solution.py:23
  166.2 23.9 %collective-permute-start.237 = (bf16[144,1280]{1,0:T(8,128)(2,1)}, bf16[144,1280]{1,0:T(8,128)(2,1)S(1)}, u32[]{:S(2)}, u32[]{:S(2)}) collective-permute-start(bf16[144,1280]{1,0:T(8,128)(2,1)} %get-tuple-element.951), channel_id=1, source_target_pairs={{0,2},{1,3},{2,0},{3,1},{4,6},{5,7},{6,4},{7,5},{8,10},{9,11},{10,... | collective-permute-start | bytes 1105928 | tf_op jit(solution)/shard_map/ppermute | solution.py:23
  166.4 23.7 %collective-permute-start.238 = (bf16[144,1280]{1,0:T(8,128)(2,1)}, bf16[144,1280]{1,0:T(8,128)(2,1)S(1)}, u32[]{:S(2)}, u32[]{:S(2)}) collective-permute-start(bf16[144,1280]{1,0:T(8,128)(2,1)} %get-tuple-element.952), channel_id=1, source_target_pairs={{0,4},{1,5},{2,6},{3,7},{4,0},{5,1},{6,2},{7,3},{8,12},{9,13},{10,... | collective-permute-start | bytes 1105928 | tf_op jit(solution)/shard_map/ppermute | solution.py:23
  170.5 19.6 %collective-permute-start.239 = (bf16[144,1280]{1,0:T(8,128)(2,1)}, bf16[144,1280]{1,0:T(8,128)(2,1)S(1)}, u32[]{:S(2)}, u32[]{:S(2)}) collective-permute-start(bf16[144,1280]{1,0:T(8,128)(2,1)} %get-tuple-element.953), channel_id=1, source_target_pairs={{0,6},{1,7},{2,4},{3,5},{4,2},{5,3},{6,0},{7,1},{8,14},{9,15},{10,... | collective-permute-start | bytes 1105928 | tf_op jit(solution)/shard_map/ppermute | solution.py:23
  170.9 13.0 %collective-permute-start.241 = (bf16[144,1024]{1,0:T(8,128)(2,1)}, bf16[144,1024]{1,0:T(8,128)(2,1)S(1)}, u32[]{:S(2)}, u32[]{:S(2)}) collective-permute-start(bf16[144,1024]{1,0:T(8,128)(2,1)} %get-tuple-element.955), channel_id=1, source_target_pairs={{0,16},{1,17},{2,18},{3,19},{4,20},{5,21},{6,22},{7,23},{8,24},{9,... | collective-permute-start | bytes 884744 | tf_op jit(solution)/shard_map/ppermute | solution.py:23
  176.1 14.0 %collective-permute-start.242 = (bf16[144,1024]{1,0:T(8,128)(2,1)}, bf16[144,1024]{1,0:T(8,128)(2,1)S(1)}, u32[]{:S(2)}, u32[]{:S(2)}) collective-permute-start(bf16[144,1024]{1,0:T(8,128)(2,1)} %get-tuple-element.956), channel_id=1, source_target_pairs={{0,24},{1,25},{2,26},{3,27},{4,28},{5,29},{6,30},{7,31},{8,16},{9,... | collective-permute-start | bytes 884744 | tf_op jit(solution)/shard_map/ppermute | solution.py:23
  191.4 9.6 %collective-permute-start.246 = (bf16[36,1024]{1,0:T(8,128)(2,1)S(1)}, bf16[36,1024]{1,0:T(8,128)(2,1)S(1)}, u32[]{:S(2)}, u32[]{:S(2)}) collective-permute-start(bf16[36,1024]{1,0:T(8,128)(2,1)S(1)} %get-tuple-element.991), channel_id=1, source_target_pairs={{0,2},{1,3},{2,0},{3,1},{4,6},{5,7},{6,4},{7,5},{8,10},{9,11},{10,... | collective-permute-start | bytes 221192 | tf_op jit(solution)/shard_map/ppermute | solution.py:23
  192.1 14.6 %collective-permute-start.243 = (bf16[36,1280]{1,0:T(8,128)(2,1)S(1)}, bf16[36,1280]{1,0:T(8,128)(2,1)S(1)}, u32[]{:S(2)}, u32[]{:S(2)}) collective-permute-start(bf16[36,1280]{1,0:T(8,128)(2,1)S(1)} %get-tuple-element.988), channel_id=1, source_target_pairs={{0,8},{1,9},{2,10},{3,11},{4,12},{5,13},{6,14},{7,15},{8,0},{9,1},... | collective-permute-start | bytes 276488 | tf_op jit(solution)/shard_map/ppermute | solution.py:23
  193.4 13.3 %collective-permute-start.244 = (bf16[36,1280]{1,0:T(8,128)(2,1)S(1)}, bf16[36,1280]{1,0:T(8,128)(2,1)S(1)}, u32[]{:S(2)}, u32[]{:S(2)}) collective-permute-start(bf16[36,1280]{1,0:T(8,128)(2,1)S(1)} %get-tuple-element.987), channel_id=1, source_target_pairs={{0,16},{1,17},{2,18},{3,19},{4,20},{5,21},{6,22},{7,23},{8,24},{9,... | collective-permute-start | bytes 276488 | tf_op jit(solution)/shard_map/ppermute | solution.py:23
  196.0 10.7 %collective-permute-start.245 = (bf16[36,1280]{1,0:T(8,128)(2,1)S(1)}, bf16[36,1280]{1,0:T(8,128)(2,1)S(1)}, u32[]{:S(2)}, u32[]{:S(2)}) collective-permute-start(bf16[36,1280]{1,0:T(8,128)(2,1)S(1)} %get-tuple-element.986), channel_id=1, source_target_pairs={{0,24},{1,25},{2,26},{3,27},{4,28},{5,29},{6,30},{7,31},{8,16},{9,... | collective-permute-start | bytes 276488 | tf_op jit(solution)/shard_map/ppermute | solution.py:23
  196.9 6.5 %collective-permute-start.247 = (bf16[36,1024]{1,0:T(8,128)(2,1)S(1)}, bf16[36,1024]{1,0:T(8,128)(2,1)S(1)}, u32[]{:S(2)}, u32[]{:S(2)}) collective-permute-start(bf16[36,1024]{1,0:T(8,128)(2,1)S(1)} %get-tuple-element.990), channel_id=1, source_target_pairs={{0,4},{1,5},{2,6},{3,7},{4,0},{5,1},{6,2},{7,3},{8,12},{9,13},{10,... | collective-permute-start | bytes 221192 | tf_op jit(solution)/shard_map/ppermute | solution.py:23
  201.0 5.7 %collective-permute-start.248 = (bf16[36,1024]{1,0:T(8,128)(2,1)S(1)}, bf16[36,1024]{1,0:T(8,128)(2,1)S(1)}, u32[]{:S(2)}, u32[]{:S(2)}) collective-permute-start(bf16[36,1024]{1,0:T(8,128)(2,1)S(1)} %get-tuple-element.989), channel_id=1, source_target_pairs={{0,6},{1,7},{2,4},{3,5},{4,2},{5,3},{6,0},{7,1},{8,14},{9,15},{10,... | collective-permute-start | bytes 221192 | tf_op jit(solution)/shard_map/ppermute | solution.py:23
  207.0 10.6 %collective-permute-start.252 = (bf16[9,1152]{1,0:T(8,128)(2,1)S(1)}, bf16[9,1152]{1,0:T(8,128)(2,1)S(1)}, u32[]{:S(2)}, u32[]{:S(2)}) collective-permute-start(bf16[9,1152]{1,0:T(8,128)(2,1)S(1)} %get-tuple-element.999), channel_id=1, source_target_pairs={{0,128},{1,129},{2,130},{3,131},{4,132},{5,133},{6,134},{7,135},{8... | collective-permute-start | bytes 62216 | tf_op jit(solution)/shard_map/ppermute | solution.py:23
  211.4 7.5 %collective-permute-start.253 = (bf16[9,1152]{1,0:T(8,128)(2,1)S(1)}, bf16[9,1152]{1,0:T(8,128)(2,1)S(1)}, u32[]{:S(2)}, u32[]{:S(2)}) collective-permute-start(bf16[9,1152]{1,0:T(8,128)(2,1)S(1)} %get-tuple-element.1002), channel_id=1, source_target_pairs={{0,160},{1,161},{2,162},{3,163},{4,164},{5,165},{6,166},{7,167},{8... | collective-permute-start | bytes 62216 | tf_op jit(solution)/shard_map/ppermute | solution.py:23
  211.5 9.3 %collective-permute-start.254 = (bf16[9,1152]{1,0:T(8,128)(2,1)S(1)}, bf16[9,1152]{1,0:T(8,128)(2,1)S(1)}, u32[]{:S(2)}, u32[]{:S(2)}) collective-permute-start(bf16[9,1152]{1,0:T(8,128)(2,1)S(1)} %get-tuple-element.1001), channel_id=1, source_target_pairs={{0,192},{1,193},{2,194},{3,195},{4,196},{5,197},{6,198},{7,199},{8... | collective-permute-start | bytes 62216 | tf_op jit(solution)/shard_map/ppermute | solution.py:23
  215.9 5.2 %collective-permute-start.255 = (bf16[9,1152]{1,0:T(8,128)(2,1)S(1)}, bf16[9,1152]{1,0:T(8,128)(2,1)S(1)}, u32[]{:S(2)}, u32[]{:S(2)}) collective-permute-start(bf16[9,1152]{1,0:T(8,128)(2,1)S(1)} %get-tuple-element.1000), channel_id=1, source_target_pairs={{0,224},{1,225},{2,226},{3,227},{4,228},{5,229},{6,230},{7,231},{8... | collective-permute-start | bytes 62216 | tf_op jit(solution)/shard_map/ppermute | solution.py:23
  216.2 4.9 %collective-permute-start.249 = (bf16[9,1152]{1,0:T(8,128)(2,1)S(1)}, bf16[9,1152]{1,0:T(8,128)(2,1)S(1)}, u32[]{:S(2)}, u32[]{:S(2)}) collective-permute-start(bf16[9,1152]{1,0:T(8,128)(2,1)S(1)} %get-tuple-element.996), channel_id=1, source_target_pairs={{0,32},{1,33},{2,34},{3,35},{4,36},{5,37},{6,38},{7,39},{8,40},{9,... | collective-permute-start | bytes 62216 | tf_op jit(solution)/shard_map/ppermute | solution.py:23
  217.5 5.3 %collective-permute-start.250 = (bf16[9,1152]{1,0:T(8,128)(2,1)S(1)}, bf16[9,1152]{1,0:T(8,128)(2,1)S(1)}, u32[]{:S(2)}, u32[]{:S(2)}) collective-permute-start(bf16[9,1152]{1,0:T(8,128)(2,1)S(1)} %get-tuple-element.998), channel_id=1, source_target_pairs={{0,64},{1,65},{2,66},{3,67},{4,68},{5,69},{6,70},{7,71},{8,72},{9,... | collective-permute-start | bytes 62216 | tf_op jit(solution)/shard_map/ppermute | solution.py:23
  218.8 5.8 %collective-permute-start.251 = (bf16[9,1152]{1,0:T(8,128)(2,1)S(1)}, bf16[9,1152]{1,0:T(8,128)(2,1)S(1)}, u32[]{:S(2)}, u32[]{:S(2)}) collective-permute-start(bf16[9,1152]{1,0:T(8,128)(2,1)S(1)} %get-tuple-element.997), channel_id=1, source_target_pairs={{0,96},{1,97},{2,98},{3,99},{4,100},{5,101},{6,102},{7,103},{8,104... | collective-permute-start | bytes 62216 | tf_op jit(solution)/shard_map/ppermute | solution.py:23
